TPU v7x, 32 devices: a whole 2x2x4 slice. The times are simulated.
32 devices in a mesh: parts: 2 (over x), coord: 16 (over z, y, core).
Axes of the slice: x: 2, y: 2, z: 4, core: 2. Of those that a mesh axis runs over, the one named last changes fastest.
Arguments:
- shape_data: bfloat16 [128, 50, 6144], P('parts', None, 'coord'), parts along dimension 0, may hold values from -6 to 6
- frame_factor: bfloat16 [100, 16], P('parts'), parts along dimension 0, may hold values from -0.875 to 0.875
- coord_factor: bfloat16 [12288, 256], P(('parts', 'coord')), parts along dimension 0, may hold values from -0.078125 to 0.078125
- subject_factor: bfloat16 [128, 128], P(('parts', 'coord')), parts along dimension 0, may hold values from -6 to 6
Outputs:
- subject_update: float32 [128, 128], P(('parts', 'coord')), parts along dimension 0
There are 2 independent parts, one for each index of `parts`. A program takes and returns all parts, laid end to end along the dimension named above; each array names one. Nothing has to cross between parts.
All inputs are finite; a program needn't handle non-finite values.
Results may differ from a plain program's by a relative error of at most 0.00088.
Values may be sent and summed in bfloat16 or wider, within the bound.
A program may use at most 64 MiB of HBM per device.

v0:
```python
import jax
import jax.numpy as jnp
from jax import lax
from jax.sharding import PartitionSpec as P


def body(shape_data, frame_factor, coord_factor, subject_factor):
    ranks_three = coord_factor.shape[1]
    ranks_two = frame_factor.shape[1]
    own_rows = subject_factor.shape[0]
    width = shape_data.shape[2]
    mixed = jnp.einsum(
        "sfc,fq->sqc", shape_data, frame_factor, preferred_element_type=jnp.float32
    ).astype(jnp.bfloat16)
    block = mixed.reshape(lax.axis_size("coord") * own_rows * ranks_two, width)
    term = jnp.dot(block, coord_factor, preferred_element_type=jnp.float32)
    core_sum = lax.psum_scatter(
        term.reshape(lax.axis_size("coord") * own_rows, ranks_two * ranks_three),
        "coord",
        scatter_dimension=0,
        tiled=True,
    )
    core_panel = core_sum.astype(jnp.bfloat16)
    scale = 1.0 / (ranks_two * ranks_three)
    panel_piece = lax.all_gather(core_panel, "coord", axis=0, tiled=True)
    factor_piece = lax.all_gather(subject_factor, "coord", axis=0, tiled=True)
    gram_block = (
        lax.dot_general(
            core_panel, panel_piece, (((1,), (1,)), ((), ())), preferred_element_type=jnp.float32
        )
        * scale
    )
    return jnp.dot(gram_block, factor_piece.astype(jnp.float32), precision=lax.Precision.HIGHEST)


def solution(mesh):
    in_specs = (
        P("parts", None, "coord"),
        P("parts", None),
        P(("parts", "coord"), None),
        P(("parts", "coord"), None),
    )
    out_specs = P(("parts", "coord"), None)
    return jax.shard_map(body, mesh=mesh, in_specs=in_specs, out_specs=out_specs, check_vma=False)
```

profile of v0, /device:TPU:0, one launch (start us, length us, event | category | flops | bytes accessed | tf_op | source)
XLA Modules:
  0.0 122.9 jit_solution(2316966170208686734)
XLA Ops:
  0.0 0.0 copy-start
  0.0 0.0 copy-start.2
  0.0 1.7 %copy-done = bf16[64,50,384]{2,0,1:T(8,128)(2,1)S(1)} copy-done((bf16[64,50,384]{2,0,1:T(8,128)(2,1)S(1)}, bf16[64,50,384]{2,0,1:T(8,128)(2,1)}, u32[]{:S(2)}) %copy-start) | copy-done | bytes 2457624
  1.7 2.7 %fusion.2 = bf16[16,64,384]{2,0,1:T(8,128)(2,1)S(1)} fusion(bf16[64,50,384]{2,0,1:T(8,128)(2,1)S(1)} %copy-done, bf16[50,16]{0,1:T(8,128)(2,1)} %param.5), kind=kOutput, calls=%fused_computation.2 | convolution fusion | flops 39714816 | bytes 3245632 | tf_op jit(solution)/shard_map/sfc,fq->sqc/dot_general | solution.py:12
  4.4 0.0 copy-done.2
  4.4 0.0 copy-start.4
  4.4 0.4 fusion.8
  4.8 0.0 copy-start.3
  4.8 1.2 reshape.7
  6.0 75.4 %all-reduce.2 = bf16[64,4096]{1,0:T(8,128)(2,1)S(1)} all-reduce(f32[64,4096]{1,0:T(8,128)} %reshape.7), channel_id=2, replica_groups=mesh['parts'=2,'coord'=16] {'coord'}, use_global_device_ids=true, to_apply=%region_0.0.clone | all-reduce | flops 262144 | bytes 1572864
  81.4 0.0 copy-start.1
  81.4 0.0 copy-done.4
  81.4 0.7 dynamic-slice
  82.7 0.0 copy-done.1
  82.7 18.7 %all-gather = bf16[16,4,4096]{2,1,0:T(4,128)(2,1)S(1)} all-gather(bf16[1,4,4096]{2,1,0:T(4,128)(2,1)S(1)} %fusion.5), channel_id=1, replica_groups=mesh['parts'=2,'coord'=16] {'coord'}, dimensions={0}, use_global_device_ids=true | all-gather | bytes 557056 | tf_op jit(solution)/shard_map/all_gather | solution.py:25
  101.5 0.1 reshape.9
  101.6 1.1 convolution_multiply_fusion
  102.7 0.0 copy-done.3
  102.7 19.5 %all-gather.1 = bf16[16,4,128]{2,1,0:T(4,128)(2,1)S(1)} all-gather(bf16[1,4,128]{2,1,0:T(4,128)(2,1)S(1)} %bitcast.18), channel_id=1, replica_groups=mesh['parts'=2,'coord'=16] {'coord'}, dimensions={0}, use_global_device_ids=true | all-gather | bytes 17408 | tf_op jit(solution)/shard_map/all_gather | solution.py:26
  122.2 0.7 fusion.9
  (1 shorter events, 0.0 us)
Async XLA Ops:
  0.0 1.7 %copy-start = (bf16[64,50,384]{2,0,1:T(8,128)(2,1)S(1)}, bf16[64,50,384]{2,0,1:T(8,128)(2,1)}, u32[]{:S(2)}) copy-start(bf16[64,50,384]{2,0,1:T(8,128)(2,1)} %param.4) | copy-start | bytes 7372804
  0.0 4.4 %copy-start.2 = (bf16[384,256]{1,0:T(8,128)(2,1)S(1)}, bf16[384,256]{1,0:T(8,128)(2,1)}, u32[]{:S(2)}) copy-start(bf16[384,256]{1,0:T(8,128)(2,1)} %param.6) | copy-start | bytes 589828
  4.4 77.0 %copy-start.4 = (u32[32]{0:T(128)S(1)}, u32[32]{0:T(128)}, u32[]{:S(2)}) copy-start(u32[32]{0:T(128)} %constant.5) | copy-start | bytes 388
  4.8 97.8 %copy-start.3 = (bf16[4,128]{1,0:T(4,128)(2,1)S(1)}, bf16[4,128]{1,0:T(4,128)(2,1)}, u32[]{:S(2)}) copy-start(bf16[4,128]{1,0:T(4,128)(2,1)} %param.7) | copy-start | bytes 3076
  81.4 1.4 %copy-start.1 = (bf16[64,4096]{1,0:T(8,128)(2,1)}, bf16[64,4096]{1,0:T(8,128)(2,1)S(1)}, u32[]{:S(2)}) copy-start(bf16[64,4096]{1,0:T(8,128)(2,1)S(1)} %all-reduce.2) | copy-start | bytes 1572868
where the time goes:
time: 123 us
  blocking collectives  114 us (93%)
  matrix products  4.91 us (4%)
  local copies, waits for them, and re-layouts  3.68 us (3%)
    unnamed x1, blocking collectives  75.4 us
    all_gather x1, blocking collectives, body(): factor_piece = lax.all_gather(subject_factor, 'coord', axis=0, tiled=True)  19.5 us
    all_gather x1, blocking collectives, body(): panel_piece = lax.all_gather(core_panel, 'coord', axis=0, tiled=True)  18.7 us
    dot_general x1, matrix products, body(): jnp.einsum('sfc,fq->sqc', shape_data, frame_factor, preferred_element_typ...  2.7 us
    unnamed x13, local copies, waits for them, and re-layouts  2.51 us

commit v1 on v0

v1 whole, which is shorter than its diff:
```python
import functools

import jax
import jax.numpy as jnp
from jax import lax
from jax.experimental import pallas as pl
from jax.experimental.pallas import tpu as pltpu
from jax.sharding import PartitionSpec as P

MESH = pl.DeviceIdType.MESH
F32 = jnp.float32
BF16 = jnp.bfloat16
GROUP = 16
CHUNKS = 4


def kernel(
    n,
    data_hbm,
    frame_hbm,
    coord_hbm,
    subject_hbm,
    out_ref,
    data,
    frame,
    coord,
    subject,
    own1,
    send1,
    recv1,
    own2,
    send2,
    recv2,
    send3,
    recv3,
    core_block,
    factor_slots,
    factor,
    update,
    update_send,
    update_recv,
    data_sem,
    small_sem,
    s1_sem,
    r1_sem,
    s2_sem,
    r2_sem,
    s3_sem,
    r3_sem,
    sf_sem,
    rf_sem,
    su_sem,
    ru_sem,
):
    part = lax.axis_index("parts")
    me = lax.axis_index("coord")
    core = lax.rem(me, 2)
    lo = lax.rem(lax.div(me, 2), 2)
    hi = lax.div(me, 4)
    nhi = n // 4
    frames, subjects, width = data.shape
    ranks_two = frame.shape[1]
    ranks_three = coord.shape[1]
    own_rows = subject.shape[0]
    rows = subjects // CHUNKS
    cols = ranks_two * ranks_three // n
    piece = min(cols, ranks_three)

    def remote(src, dst, send, recv, target):
        return pltpu.make_async_remote_copy(
            src_ref=src,
            dst_ref=dst,
            send_sem=send,
            recv_sem=recv,
            device_id=(part, target),
            device_id_type=MESH,
        )

    small = [
        pltpu.make_async_copy(frame_hbm, frame, small_sem.at[0]),
        pltpu.make_async_copy(coord_hbm, coord, small_sem.at[1]),
        pltpu.make_async_copy(subject_hbm, subject, small_sem.at[2]),
    ]
    loads = [
        pltpu.make_async_copy(
            data_hbm.at[:, pl.ds(k * rows, rows), :],
            data.at[:, pl.ds(k * rows, rows), :],
            data_sem.at[k],
        )
        for k in range(CHUNKS)
    ]
    small[0].start()
    loads[0].start()
    small[1].start()
    small[2].start()
    for k in range(1, CHUNKS):
        loads[k].start()

    barrier = pltpu.get_barrier_semaphore()
    for j in range(1, n):
        pl.semaphore_signal(
            barrier, inc=1, device_id=(part, lax.rem(me + j, n)), device_id_type=MESH
        )

    small[0].wait()
    tall = ranks_two * GROUP
    deep = frames * GROUP
    pick_q = (
        lax.broadcasted_iota(jnp.int32, (tall, ranks_two), 0) // GROUP
        == lax.broadcasted_iota(jnp.int32, (tall, ranks_two), 1)
    )
    pick_f = (
        lax.broadcasted_iota(jnp.int32, (frames, deep), 1) // GROUP
        == lax.broadcasted_iota(jnp.int32, (frames, deep), 0)
    )
    by_q = lax.dot_general(
        jnp.where(pick_q, 1.0, 0.0).astype(BF16),
        frame[...],
        (((1,), (1,)), ((), ())),
        preferred_element_type=F32,
    ).astype(BF16)
    spread = jnp.dot(by_q, jnp.where(pick_f, 1.0, 0.0).astype(BF16), preferred_element_type=F32)
    same = (
        lax.broadcasted_iota(jnp.int32, (tall, deep), 0) % GROUP
        == lax.broadcasted_iota(jnp.int32, (tall, deep), 1) % GROUP
    )
    weights = jnp.where(same, spread, 0.0).astype(BF16)

    small[1].wait()
    coord_value = coord[...]

    def compute(k):
        for g in range(rows // GROUP):
            first = k * rows + g * GROUP
            block = data[:, first : first + GROUP, :].reshape(deep, width)
            mixed = jnp.dot(weights, block, preferred_element_type=F32).astype(BF16)
            term = jnp.dot(mixed, coord_value, preferred_element_type=F32)
            pieces = {}
            for q in range(ranks_two):
                for b in range(ranks_three // piece):
                    start = q * ranks_three + b * piece
                    pieces[start // cols, start % cols] = term[
                        q * GROUP : (q + 1) * GROUP, b * piece : (b + 1) * piece
                    ]
            for (owner, at), zero in pieces.items():
                if owner % 2:
                    continue
                one = pieces[owner + 1, at]
                l, h = owner // 2 % 2, owner // 4
                own1[l, h, first : first + GROUP, at : at + piece] = jnp.where(core == 0, zero, one)
                send1[k, l, h, g * GROUP : (g + 1) * GROUP, at : at + piece] = jnp.where(
                    core == 0, one, zero
                ).astype(BF16)

    sends = []

    def begin(copy):
        copy.start()
        sends.append(copy)

    first_copies = [
        remote(send1.at[k], recv1.at[k], s1_sem.at[k], r1_sem.at[k], me + 1 - 2 * core)
        for k in range(CHUNKS)
    ]
    second_copies = [
        remote(send2.at[k], recv2.at[k], s2_sem.at[k], r2_sem.at[k], me + 2 - 4 * lo)
        for k in range(CHUNKS)
    ]
    third_copies = [
        [
            remote(
                send3.at[k, j - 1],
                recv3.at[k, j - 1],
                s3_sem.at[k, j - 1],
                r3_sem.at[k, j - 1],
                lax.rem(hi + j, nhi) * 4 + lo * 2 + core,
            )
            for j in range(1, nhi)
        ]
        for k in range(CHUNKS)
    ]
    factor_copies = [
        remote(
            factor_slots.at[me],
            factor_slots.at[me],
            sf_sem.at[j - 1],
            rf_sem.at[j - 1],
            lax.rem(me + j, n),
        )
        for j in range(1, n)
    ]
    update_copies = [
        remote(
            update_send.at[lax.rem(me + j, n)],
            update_recv.at[j - 1],
            su_sem.at[j - 1],
            ru_sem.at[j - 1],
            lax.rem(me + j, n),
        )
        for j in range(1, n)
    ]

    def second(k):
        first_copies[k].wait_recv()
        at = pl.ds(k * rows, rows)
        send2[k] = (own1[1 - lo, :, at, :] + recv1[k, 1 - lo].astype(F32)).astype(BF16)
        begin(second_copies[k])
        own2[:, at, :] = own1[lo, :, at, :] + recv1[k, lo].astype(F32)

    def third(k):
        second_copies[k].wait_recv()
        at = pl.ds(k * rows, rows)
        for j in range(1, nhi):
            there = lax.rem(hi + j, nhi)
            send3[k, j - 1] = (own2[there, at, :] + recv2[k, there].astype(F32)).astype(BF16)
            begin(third_copies[k][j - 1])

    def fourth(k):
        at = pl.ds(k * rows, rows)
        total = own2[hi, at, :] + recv2[k, hi].astype(F32)
        for j in range(1, nhi):
            third_copies[k][j - 1].wait_recv()
            total += recv3[k, j - 1].astype(F32)
        core_block[at, :] = total.astype(BF16)

    for step in range(CHUNKS + 2):
        if step < CHUNKS:
            loads[step].wait()
            compute(step)
            if step == 0:
                pl.semaphore_wait(barrier, n - 1)
            begin(first_copies[step])
        if 1 <= step <= CHUNKS:
            second(step - 1)
        if 2 <= step:
            third(step - 2)
        if step == 1:
            small[2].wait()
            factor_slots[me] = subject[...].astype(F32)
            for copy in factor_copies:
                begin(copy)
    for copy in factor_copies:
        copy.wait_recv()
    for d in range(n):
        factor[d * own_rows : (d + 1) * own_rows, :] = factor_slots[d]
    for k in range(CHUNKS):
        fourth(k)

    panel = core_block[...]
    gram = lax.dot_general(
        panel, panel, (((1,), (1,)), ((), ())), preferred_element_type=F32
    ) * (1.0 / (ranks_two * ranks_three))
    top = gram.astype(BF16)
    rest = gram - top.astype(F32)
    middle = rest.astype(BF16)
    low = (rest - middle.astype(F32)).astype(BF16)
    stacked = jnp.concatenate([top, middle, low], axis=0)
    product = jnp.dot(stacked, factor[...].astype(BF16), preferred_element_type=F32)
    update[...] = (
        product[:subjects] + (product[subjects : 2 * subjects] + product[2 * subjects :])
    )
    for d in range(n):
        update_send[d] = update[d * own_rows : (d + 1) * own_rows, :]
    for copy in update_copies:
        begin(copy)
    total = update_send[me]
    for j in range(1, n):
        update_copies[j - 1].wait_recv()
        total += update_recv[j - 1]
    out_ref[...] = total
    for copy in sends:
        copy.wait_send()


def body(shape_data, frame_factor, coord_factor, subject_factor):
    n = lax.axis_size("coord")
    subjects, frames, width = shape_data.shape
    ranks_two = frame_factor.shape[1]
    ranks_three = coord_factor.shape[1]
    own_rows, ranks_one = subject_factor.shape
    nhi = n // 4
    rows = subjects // CHUNKS
    cols = ranks_two * ranks_three // n
    dma = pltpu.SemaphoreType.DMA
    return pl.pallas_call(
        functools.partial(kernel, n),
        out_shape=jax.ShapeDtypeStruct((own_rows, ranks_one), F32),
        in_specs=[pl.BlockSpec(memory_space=pl.ANY)] * 4,
        out_specs=pl.BlockSpec(memory_space=pltpu.VMEM),
        scratch_shapes=[
            pltpu.VMEM((frames, subjects, width), BF16),
            pltpu.VMEM(frame_factor.shape, BF16),
            pltpu.VMEM(coord_factor.shape, BF16),
            pltpu.VMEM(subject_factor.shape, BF16),
            pltpu.VMEM((2, nhi, subjects, cols), F32),
            pltpu.VMEM((CHUNKS, 2, nhi, rows, cols), BF16),
            pltpu.VMEM((CHUNKS, 2, nhi, rows, cols), BF16),
            pltpu.VMEM((nhi, subjects, cols), F32),
            pltpu.VMEM((CHUNKS, nhi, rows, cols), BF16),
            pltpu.VMEM((CHUNKS, nhi, rows, cols), BF16),
            pltpu.VMEM((CHUNKS, nhi - 1, rows, cols), BF16),
            pltpu.VMEM((CHUNKS, nhi - 1, rows, cols), BF16),
            pltpu.VMEM((subjects, cols), BF16),
            pltpu.VMEM((n, own_rows, ranks_one), F32),
            pltpu.VMEM((subjects, ranks_one), F32),
            pltpu.VMEM((subjects, ranks_one), F32),
            pltpu.VMEM((n, own_rows, ranks_one), F32),
            pltpu.VMEM((n - 1, own_rows, ranks_one), F32),
            dma((CHUNKS,)),
            dma((3,)),
            dma((CHUNKS,)),
            dma((CHUNKS,)),
            dma((CHUNKS,)),
            dma((CHUNKS,)),
            dma((CHUNKS, nhi - 1)),
            dma((CHUNKS, nhi - 1)),
            dma((n - 1,)),
            dma((n - 1,)),
            dma((n - 1,)),
            dma((n - 1,)),
        ],
        compiler_params=pltpu.CompilerParams(
            collective_id=0, has_side_effects=True, vmem_limit_bytes=48 * 1024 * 1024
        ),
    )(jnp.transpose(shape_data, (1, 0, 2)), frame_factor, coord_factor, subject_factor)


def solution(mesh):
    in_specs = (
        P("parts", None, "coord"),
        P("parts", None),
        P(("parts", "coord"), None),
        P(("parts", "coord"), None),
    )
    out_specs = P(("parts", "coord"), None)
    return jax.shard_map(body, mesh=mesh, in_specs=in_specs, out_specs=out_specs, check_vma=False)
```

time: 123 us -> 28.4 us (0.23)
  blocking collectives: 114 us -> 0 us
  Pallas kernels: 0 us -> 23.5 us
  matrix products: 4.91 us -> 0 us
    unnamed x1 -> x0, blocking collectives: 75.4 us -> none
    all_gather x2 -> x0, blocking collectives: 38.2 us -> none  [the longest x1 19.5 us: body(): factor_piece = lax.all_gather(subject_factor, 'coord', axis=0, tiled=True)]
    pallas_call x0 -> x1, Pallas kernels: none -> 23.5 us  [body(): pl.pallas_call(functools.partial(kernel, n), out_shape=jax.ShapeDtypeStru...]
    dot_general x4 -> x0, matrix products: 4.91 us -> none  [the longest x1 2.7 us: body(): jnp.einsum('sfc,fq->sqc', shape_data, frame_factor, preferred_element_typ...]
    unnamed x13 -> x8, local copies, waits for them, and re-layouts: 2.51 us -> 4.67 us
where the time goes in v1:
time: 28.4 us; the launch traced here: 28.2 us
  Pallas kernels  23.5 us (83%)
  local copies, waits for them, and re-layouts  4.67 us (16%)
    pallas_call x1, Pallas kernels, body(): pl.pallas_call(functools.partial(kernel, n), out_shape=jax.ShapeDtypeStru...  23.5 us
    unnamed x8, local copies, waits for them, and re-layouts  4.67 us

profile of v1, /device:TPU:0, one launch (start us, length us, event | category | flops | bytes accessed | tf_op | source)
XLA Modules:
  0.0 28.2 jit_solution(6349468792123228493)
XLA Ops:
  0.0 0.8 %copy.5.frame_hbm = bf16[50,16]{1,0:T(8,128)(2,1)S(1)} copy(bf16[50,16]{0,1:T(8,128)(2,1)} %param.5) | data formatting | bytes 3200 | tf_op args[1]
  0.8 0.0 copy-start
  0.8 1.7 %copy-done = bf16[64,50,384]{2,0,1:T(8,128)(2,1)S(1)} copy-done((bf16[64,50,384]{2,0,1:T(8,128)(2,1)S(1)}, bf16[64,50,384]{2,0,1:T(8,128)(2,1)}, u32[]{:S(2)}) %copy-start) | copy-done | bytes 2457624
  2.5 0.0 copy-start.1
  2.5 0.9 %copy-done.1 = bf16[384,256]{1,0:T(8,128)(2,1)S(1)} copy-done((bf16[384,256]{1,0:T(8,128)(2,1)S(1)}, bf16[384,256]{1,0:T(8,128)(2,1)}, u32[]{:S(2)}) %copy-start.1) | copy-done | bytes 196632
  3.4 0.0 copy-start.2
  3.4 0.7 %copy-done.2 = bf16[4,128]{1,0:T(4,128)(2,1)S(1)} copy-done((bf16[4,128]{1,0:T(4,128)(2,1)S(1)}, bf16[4,128]{1,0:T(4,128)(2,1)}, u32[]{:S(2)}) %copy-start.2) | copy-done | bytes 1048
  4.1 23.5 %shard_map.46 = f32[4,128]{1,0:T(4,128)S(1)} custom-call(bf16[50,64,384]{2,1,0:T(8,128)(2,1)S(1)} %bitcast.1, bf16[50,16]{1,0:T(8,128)(2,1)S(1)} %copy.5.frame_hbm, bf16[384,256]{1,0:T(8,128)(2,1)S(1)} %copy-done.1, bf16[4,128]{1,0:T(4,128)(2,1)S(1)} %copy-done.2), custom_call_target="tpu_custom_call" | custom-call | tf_op jit(solution)/shard_map/pallas_call | solution.py:285
  27.6 0.6 %copy.7 = f32[4,128]{1,0:T(4,128)} copy(f32[4,128]{1,0:T(4,128)S(1)} %shard_map.46) | data formatting | bytes 4096
Async XLA Ops:
  0.8 1.7 %copy-start = (bf16[64,50,384]{2,0,1:T(8,128)(2,1)S(1)}, bf16[64,50,384]{2,0,1:T(8,128)(2,1)}, u32[]{:S(2)}) copy-start(bf16[64,50,384]{2,0,1:T(8,128)(2,1)} %param.4) | copy-start | bytes 7372804
  2.5 0.9 %copy-start.1 = (bf16[384,256]{1,0:T(8,128)(2,1)S(1)}, bf16[384,256]{1,0:T(8,128)(2,1)}, u32[]{:S(2)}) copy-start(bf16[384,256]{1,0:T(8,128)(2,1)} %coord_hbm.1) | copy-start | bytes 589828
  3.4 0.7 %copy-start.2 = (bf16[4,128]{1,0:T(4,128)(2,1)S(1)}, bf16[4,128]{1,0:T(4,128)(2,1)}, u32[]{:S(2)}) copy-start(bf16[4,128]{1,0:T(4,128)(2,1)} %subject_hbm.1) | copy-start | bytes 3076

commit v2 on v1

v2 whole, which is shorter than its diff:
```python
import functools

import jax
import jax.numpy as jnp
from jax import lax
from jax.experimental import pallas as pl
from jax.experimental.pallas import tpu as pltpu
from jax.sharding import PartitionSpec as P

MESH = pl.DeviceIdType.MESH
F32 = jnp.float32
BF16 = jnp.bfloat16
GROUP = 16
LOADS = 4
CHUNKS = 2


def kernel(
    n,
    data_hbm,
    frame_hbm,
    coord_hbm,
    subject_hbm,
    out_ref,
    data,
    frame,
    coord,
    subject,
    own,
    send1,
    recv1,
    send2,
    recv2,
    core_block,
    factor_slots,
    factor,
    update,
    update_send,
    update_recv,
    data_sem,
    small_sem,
    s1_sem,
    r1_sem,
    s2_sem,
    r2_sem,
    sf_sem,
    rf_sem,
    su_sem,
    ru_sem,
):
    part = lax.axis_index("parts")
    me = lax.axis_index("coord")
    core = lax.rem(me, 2)
    chip = lax.div(me, 2)
    chips = n // 2
    frames, subjects, width = data.shape
    ranks_two = frame.shape[0]
    ranks_three = coord.shape[1]
    own_rows = subject.shape[0]
    load_rows = subjects // LOADS
    rows = subjects // CHUNKS
    cols = ranks_two * ranks_three // n
    piece = min(cols, ranks_three)

    def partner(index, mask):
        bit = 1
        while bit <= mask:
            if mask & bit:
                index = index + bit - 2 * bit * lax.rem(lax.div(index, bit), 2)
            bit *= 2
        return index

    def remote(src, dst, send, recv, target):
        return pltpu.make_async_remote_copy(
            src_ref=src,
            dst_ref=dst,
            send_sem=send,
            recv_sem=recv,
            device_id=(part, target),
            device_id_type=MESH,
        )

    barrier = pltpu.get_barrier_semaphore()
    for mask in range(n - 1, 0, -1):
        pl.semaphore_signal(
            barrier, inc=1, device_id=(part, partner(me, mask)), device_id_type=MESH
        )

    small = [
        pltpu.make_async_copy(frame_hbm, frame, small_sem.at[0]),
        pltpu.make_async_copy(coord_hbm, coord, small_sem.at[1]),
        pltpu.make_async_copy(subject_hbm, subject, small_sem.at[2]),
    ]
    loads = [
        pltpu.make_async_copy(
            data_hbm.at[:, pl.ds(k * load_rows, load_rows), :],
            data.at[:, pl.ds(k * load_rows, load_rows), :],
            data_sem.at[k],
        )
        for k in range(LOADS)
    ]
    small[0].start()
    loads[0].start()
    small[1].start()
    small[2].start()
    for k in range(1, LOADS):
        loads[k].start()

    small[0].wait()
    tall = ranks_two * GROUP
    deep = frames * GROUP
    pick_q = (
        lax.broadcasted_iota(jnp.int32, (tall, ranks_two), 0) // GROUP
        == lax.broadcasted_iota(jnp.int32, (tall, ranks_two), 1)
    )
    pick_f = (
        lax.broadcasted_iota(jnp.int32, (frames, deep), 1) // GROUP
        == lax.broadcasted_iota(jnp.int32, (frames, deep), 0)
    )
    by_q = jnp.dot(
        jnp.where(pick_q, 1.0, 0.0).astype(BF16), frame[...], preferred_element_type=F32
    ).astype(BF16)
    spread = jnp.dot(by_q, jnp.where(pick_f, 1.0, 0.0).astype(BF16), preferred_element_type=F32)
    same = (
        lax.broadcasted_iota(jnp.int32, (tall, deep), 0) % GROUP
        == lax.broadcasted_iota(jnp.int32, (tall, deep), 1) % GROUP
    )
    weights = jnp.where(same, spread, 0.0).astype(BF16)

    small[1].wait()
    coord_value = coord[...]

    def compute(first):
        block = data[:, first : first + GROUP, :].reshape(deep, width)
        mixed = jnp.dot(weights, block, preferred_element_type=F32).astype(BF16)
        term = jnp.dot(mixed, coord_value, preferred_element_type=F32)
        pieces = {}
        for q in range(ranks_two):
            for b in range(ranks_three // piece):
                start = q * ranks_three + b * piece
                pieces[start // cols, start % cols] = term[
                    q * GROUP : (q + 1) * GROUP, b * piece : (b + 1) * piece
                ]
        chunk, at = first // rows, first % rows
        for (owner, left), zero in pieces.items():
            if owner % 2:
                continue
            one = pieces[owner + 1, left]
            own[owner // 2, first : first + GROUP, left : left + piece] = jnp.where(
                core == 0, zero, one
            )
            send1[chunk, owner // 2, at : at + GROUP, left : left + piece] = jnp.where(
                core == 0, one, zero
            ).astype(send1.dtype)

    sends = []

    def begin(copy):
        copy.start()
        sends.append(copy)

    sibling_copies = [
        remote(send1.at[k], recv1.at[k], s1_sem.at[k], r1_sem.at[k], partner(me, 1))
        for k in range(CHUNKS)
    ]
    chip_copies = [
        {
            mask: remote(
                send2.at[k, mask - 1],
                recv2.at[k, mask - 1],
                s2_sem.at[k, mask - 1],
                r2_sem.at[k, mask - 1],
                partner(me, 2 * mask),
            )
            for mask in range(chips - 1, 0, -1)
        }
        for k in range(CHUNKS)
    ]
    factor_copies = [
        remote(
            factor_slots.at[me],
            factor_slots.at[me],
            sf_sem.at[mask - 1],
            rf_sem.at[mask - 1],
            partner(me, mask),
        )
        for mask in range(n - 1, 0, -1)
    ]
    update_copies = [
        remote(
            update_send.at[partner(me, mask)],
            update_recv.at[mask - 1],
            su_sem.at[mask - 1],
            ru_sem.at[mask - 1],
            partner(me, mask),
        )
        for mask in range(n - 1, 0, -1)
    ]

    for first in range(0, subjects, GROUP):
        if first % load_rows == 0:
            loads[first // load_rows].wait()
        compute(first)
    small[2].wait()
    factor_slots[me] = subject[...].astype(F32)

    pl.semaphore_wait(barrier, n - 1)
    for copy in sibling_copies:
        begin(copy)
    for k in range(CHUNKS):
        sibling_copies[k].wait_recv()
        at = pl.ds(k * rows, rows)
        for mask, copy in chip_copies[k].items():
            there = partner(chip, mask)
            send2[k, mask - 1] = (own[there, at, :] + recv1[k, there].astype(F32)).astype(BF16)
            begin(copy)
    for copy in factor_copies:
        begin(copy)
    for copy in factor_copies:
        copy.wait_recv()
    for d in range(n):
        factor[d * own_rows : (d + 1) * own_rows, :] = factor_slots[d]
    for k in range(CHUNKS):
        at = pl.ds(k * rows, rows)
        total = own[chip, at, :] + recv1[k, chip].astype(F32)
        for mask in range(1, chips):
            chip_copies[k][mask].wait_recv()
            total += recv2[k, mask - 1].astype(F32)
        core_block[at, :] = total.astype(BF16)

    panel = core_block[...]
    gram = lax.dot_general(
        panel, panel, (((1,), (1,)), ((), ())), preferred_element_type=F32
    ) * (1.0 / (ranks_two * ranks_three))
    top = gram.astype(BF16)
    rest = gram - top.astype(F32)
    middle = rest.astype(BF16)
    low = (rest - middle.astype(F32)).astype(BF16)
    stacked = jnp.concatenate([top, middle, low], axis=0)
    product = jnp.dot(stacked, factor[...].astype(BF16), preferred_element_type=F32)
    update[...] = (
        product[:subjects] + (product[subjects : 2 * subjects] + product[2 * subjects :])
    )
    for d in range(n):
        update_send[d] = update[d * own_rows : (d + 1) * own_rows, :]
    for copy in update_copies:
        begin(copy)
    total = update_send[me]
    for copy in reversed(update_copies):
        copy.wait_recv()
    for mask in range(1, n):
        total += update_recv[mask - 1]
    out_ref[...] = total
    for copy in sends:
        copy.wait_send()


def body(shape_data, frame_factor, coord_factor, subject_factor):
    n = lax.axis_size("coord")
    subjects, frames, width = shape_data.shape
    ranks_two = frame_factor.shape[1]
    ranks_three = coord_factor.shape[1]
    own_rows, ranks_one = subject_factor.shape
    chips = n // 2
    rows = subjects // CHUNKS
    cols = ranks_two * ranks_three // n
    dma = pltpu.SemaphoreType.DMA
    return pl.pallas_call(
        functools.partial(kernel, n),
        out_shape=jax.ShapeDtypeStruct((own_rows, ranks_one), F32),
        in_specs=[pl.BlockSpec(memory_space=pl.ANY)] * 4,
        out_specs=pl.BlockSpec(memory_space=pltpu.VMEM),
        scratch_shapes=[
            pltpu.VMEM((frames, subjects, width), BF16),
            pltpu.VMEM((ranks_two, frames), BF16),
            pltpu.VMEM(coord_factor.shape, BF16),
            pltpu.VMEM(subject_factor.shape, BF16),
            pltpu.VMEM((chips, subjects, cols), F32),
            pltpu.VMEM((CHUNKS, chips, rows, cols), BF16),
            pltpu.VMEM((CHUNKS, chips, rows, cols), BF16),
            pltpu.VMEM((CHUNKS, chips - 1, rows, cols), BF16),
            pltpu.VMEM((CHUNKS, chips - 1, rows, cols), BF16),
            pltpu.VMEM((subjects, cols), BF16),
            pltpu.VMEM((n, own_rows, ranks_one), F32),
            pltpu.VMEM((subjects, ranks_one), F32),
            pltpu.VMEM((subjects, ranks_one), F32),
            pltpu.VMEM((n, own_rows, ranks_one), F32),
            pltpu.VMEM((n - 1, own_rows, ranks_one), F32),
            dma((LOADS,)),
            dma((3,)),
            dma((CHUNKS,)),
            dma((CHUNKS,)),
            dma((CHUNKS, chips - 1)),
            dma((CHUNKS, chips - 1)),
            dma((n - 1,)),
            dma((n - 1,)),
            dma((n - 1,)),
            dma((n - 1,)),
        ],
        compiler_params=pltpu.CompilerParams(
            collective_id=0, has_side_effects=True, vmem_limit_bytes=60 * 1024 * 1024
        ),
    )(jnp.transpose(shape_data, (1, 0, 2)), frame_factor.T, coord_factor, subject_factor)


def solution(mesh):
    in_specs = (
        P("parts", None, "coord"),
        P("parts", None),
        P(("parts", "coord"), None),
        P(("parts", "coord"), None),
    )
    out_specs = P(("parts", "coord"), None)
    return jax.shard_map(body, mesh=mesh, in_specs=in_specs, out_specs=out_specs, check_vma=False)
```

time: 28.4 us -> 23.8 us (0.84)
  local copies, waits for them, and re-layouts: 4.67 us -> 1.26 us
  Pallas kernels: 23.5 us -> 22.3 us
    unnamed x8 -> x1, local copies, waits for them, and re-layouts: 4.67 us -> 1.26 us
    pallas_call x1, Pallas kernels: 23.5 us -> 22.3 us  [body(): pl.pallas_call(functools.partial(kernel, n), out_shape=jax.ShapeDtypeStru...]
where the time goes in v2:
time: 23.8 us; the launch traced here: 23.6 us
  Pallas kernels  22.3 us (94%)
  local copies, waits for them, and re-layouts  1.26 us (5%)
    pallas_call x1, Pallas kernels, body(): pl.pallas_call(functools.partial(kernel, n), out_shape=jax.ShapeDtypeStru...  22.3 us
    unnamed x1, local copies, waits for them, and re-layouts  1.26 us

profile of v2, /device:TPU:0, one launch (start us, length us, event | category | flops | bytes accessed | tf_op | source)
XLA Modules:
  0.0 23.6 jit_solution(188340844232877303)
XLA Ops:
  0.0 22.3 %shard_map.46 = f32[4,128]{1,0:T(4,128)} custom-call(bf16[50,64,384]{2,1,0:T(8,128)(2,1)} %bitcast.2, bf16[16,50]{1,0:T(8,128)(2,1)} %bitcast.3, bf16[384,256]{1,0:T(8,128)(2,1)} %coord_hbm.1, bf16[4,128]{1,0:T(4,128)(2,1)} %subject_hbm.1), custom_call_target="tpu_custom_call" | custom-call | tf_op jit(solution)/shard_map/pallas_call | solution.py:268
  22.3 1.3 %copy.6 = f32[4,128]{1,0:T(4,128)} copy(f32[4,128]{1,0:T(4,128)} %shard_map.46) | data formatting | bytes 4096

commit v3 on v2

--- a/solution.py
+++ b/solution.py
@@ -29,8 +29,14 @@
     own,
     send1,
     recv1,
-    send2,
-    recv2,
+    y_send_first,
+    y_recv_first,
+    z_send_first,
+    z_recv_first,
+    y_send_last,
+    y_recv_last,
+    z_send_last,
+    z_recv_last,
     core_block,
     factor_slots,
     factor,
@@ -41,8 +47,10 @@
     small_sem,
     s1_sem,
     r1_sem,
-    s2_sem,
-    r2_sem,
+    sy_sem,
+    ry_sem,
+    sz_sem,
+    rz_sem,
     sf_sem,
     rf_sem,
     su_sem,
@@ -51,8 +59,9 @@
     part = lax.axis_index("parts")
     me = lax.axis_index("coord")
     core = lax.rem(me, 2)
-    chip = lax.div(me, 2)
-    chips = n // 2
+    lo = lax.rem(lax.div(me, 2), 2)
+    hi = lax.div(me, 4)
+    nhi = n // 4
     frames, subjects, width = data.shape
     ranks_two = frame.shape[0]
     ranks_three = coord.shape[1]
@@ -81,7 +90,8 @@
         )
 
     barrier = pltpu.get_barrier_semaphore()
-    for mask in range(n - 1, 0, -1):
+    partners = [4 * mask for mask in range(nhi - 1, 0, -1)] + [2, 1]
+    for mask in partners:
         pl.semaphore_signal(
             barrier, inc=1, device_id=(part, partner(me, mask)), device_id_type=MESH
         )
@@ -146,10 +156,11 @@
             if owner % 2:
                 continue
             one = pieces[owner + 1, left]
-            own[owner // 2, first : first + GROUP, left : left + piece] = jnp.where(
+            low, high = owner // 2 % 2, owner // 4
+            own[low, high, first : first + GROUP, left : left + piece] = jnp.where(
                 core == 0, zero, one
             )
-            send1[chunk, owner // 2, at : at + GROUP, left : left + piece] = jnp.where(
+            send1[chunk, low, high, at : at + GROUP, left : left + piece] = jnp.where(
                 core == 0, one, zero
             ).astype(send1.dtype)
 
@@ -163,28 +174,38 @@
         remote(send1.at[k], recv1.at[k], s1_sem.at[k], r1_sem.at[k], partner(me, 1))
         for k in range(CHUNKS)
     ]
-    chip_copies = [
-        {
-            mask: remote(
-                send2.at[k, mask - 1],
-                recv2.at[k, mask - 1],
-                s2_sem.at[k, mask - 1],
-                r2_sem.at[k, mask - 1],
-                partner(me, 2 * mask),
-            )
-            for mask in range(chips - 1, 0, -1)
-        }
-        for k in range(CHUNKS)
-    ]
-    factor_copies = [
-        remote(
-            factor_slots.at[me],
-            factor_slots.at[me],
-            sf_sem.at[mask - 1],
-            rf_sem.at[mask - 1],
-            partner(me, mask),
-        )
-        for mask in range(n - 1, 0, -1)
+    z_masks = range(nhi - 1, 0, -1)
+    y_first = remote(y_send_first, y_recv_first, sy_sem.at[0], ry_sem.at[0], partner(me, 2))
+    y_last = remote(y_send_last, y_recv_last, sy_sem.at[1], ry_sem.at[1], partner(me, 2))
+    z_first = {
+        mask: remote(
+            z_send_first.at[mask - 1],
+            z_recv_first.at[mask - 1],
+            sz_sem.at[0, mask - 1],
+            rz_sem.at[0, mask - 1],
+            partner(me, 4 * mask),
+        )
+        for mask in z_masks
+    }
+    z_last = {
+        mask: remote(
+            z_send_last.at[mask - 1],
+            z_recv_last.at[mask - 1],
+            sz_sem.at[1, mask - 1],
+            rz_sem.at[1, mask - 1],
+            partner(me, 4 * mask),
+        )
+        for mask in z_masks
+    }
+
+    def factor_copy(start, count, sem, target):
+        slots = factor_slots.at[pl.ds(start, count)]
+        return remote(slots, slots, sf_sem.at[sem], rf_sem.at[sem], target)
+
+    factor_sibling = factor_copy(me, 1, 0, partner(me, 1))
+    factor_y = factor_copy(me - core, 2, 1, partner(me, 2))
+    factor_z = [
+        factor_copy(hi * 4, 4, 1 + mask, partner(me, 4 * mask)) for mask in z_masks
     ]
     update_copies = [
         remote(
@@ -204,29 +225,55 @@
     small[2].wait()
     factor_slots[me] = subject[...].astype(F32)
 
-    pl.semaphore_wait(barrier, n - 1)
+    pl.semaphore_wait(barrier, len(partners))
     for copy in sibling_copies:
         begin(copy)
-    for k in range(CHUNKS):
-        sibling_copies[k].wait_recv()
-        at = pl.ds(k * rows, rows)
-        for mask, copy in chip_copies[k].items():
-            there = partner(chip, mask)
-            send2[k, mask - 1] = (own[there, at, :] + recv1[k, there].astype(F32)).astype(BF16)
-            begin(copy)
-    for copy in factor_copies:
+    begin(factor_sibling)
+    a = pl.ds(0, rows)
+    b = pl.ds(rows, rows)
+
+    sibling_copies[0].wait_recv()
+    y_send_first[...] = (own[1 - lo, :, a, :] + recv1[0, 1 - lo].astype(F32)).astype(BF16)
+    begin(y_first)
+    sibling_copies[1].wait_recv()
+    for mask in z_masks:
+        there = partner(hi, mask)
+        z_send_first[mask - 1] = (own[:, there, b, :] + recv1[1, :, there].astype(F32)).astype(BF16)
+        begin(z_first[mask])
+    factor_sibling.wait_recv()
+    begin(factor_y)
+    own[lo, :, a, :] = own[lo, :, a, :] + recv1[0, lo].astype(F32)
+    own[:, hi, b, :] = own[:, hi, b, :] + recv1[1, :, hi].astype(F32)
+
+    y_first.wait_recv()
+    for mask in z_masks:
+        there = partner(hi, mask)
+        z_send_last[mask - 1] = (own[lo, there, a, :] + y_recv_first[there].astype(F32)).astype(BF16)
+        begin(z_last[mask])
+    factor_y.wait_recv()
+    for copy in factor_z:
         begin(copy)
-    for copy in factor_copies:
+    for mask in reversed(z_masks):
+        z_first[mask].wait_recv()
+    total = own[1 - lo, hi, b, :]
+    for mask in z_masks:
+        total += z_recv_first[mask - 1, 1 - lo].astype(F32)
+    y_send_last[...] = total.astype(BF16)
+    begin(y_last)
+    total_a = own[lo, hi, a, :] + y_recv_first[hi].astype(F32)
+    total_b = own[lo, hi, b, :]
+    for mask in z_masks:
+        total_b += z_recv_first[mask - 1, lo].astype(F32)
+    for copy in factor_z:
         copy.wait_recv()
     for d in range(n):
         factor[d * own_rows : (d + 1) * own_rows, :] = factor_slots[d]
-    for k in range(CHUNKS):
-        at = pl.ds(k * rows, rows)
-        total = own[chip, at, :] + recv1[k, chip].astype(F32)
-        for mask in range(1, chips):
-            chip_copies[k][mask].wait_recv()
-            total += recv2[k, mask - 1].astype(F32)
-        core_block[at, :] = total.astype(BF16)
+    for mask in reversed(z_masks):
+        z_last[mask].wait_recv()
+        total_a += z_recv_last[mask - 1].astype(F32)
+    core_block[a, :] = total_a.astype(BF16)
+    y_last.wait_recv()
+    core_block[b, :] = (total_b + y_recv_last[...].astype(F32)).astype(BF16)
 
     panel = core_block[...]
     gram = lax.dot_general(
@@ -261,7 +308,7 @@
     ranks_two = frame_factor.shape[1]
     ranks_three = coord_factor.shape[1]
     own_rows, ranks_one = subject_factor.shape
-    chips = n // 2
+    nhi = n // 4
     rows = subjects // CHUNKS
     cols = ranks_two * ranks_three // n
     dma = pltpu.SemaphoreType.DMA
@@ -275,11 +322,17 @@
             pltpu.VMEM((ranks_two, frames), BF16),
             pltpu.VMEM(coord_factor.shape, BF16),
             pltpu.VMEM(subject_factor.shape, BF16),
-            pltpu.VMEM((chips, subjects, cols), F32),
-            pltpu.VMEM((CHUNKS, chips, rows, cols), BF16),
-            pltpu.VMEM((CHUNKS, chips, rows, cols), BF16),
-            pltpu.VMEM((CHUNKS, chips - 1, rows, cols), BF16),
-            pltpu.VMEM((CHUNKS, chips - 1, rows, cols), BF16),
+            pltpu.VMEM((2, nhi, subjects, cols), F32),
+            pltpu.VMEM((CHUNKS, 2, nhi, rows, cols), BF16),
+            pltpu.VMEM((CHUNKS, 2, nhi, rows, cols), BF16),
+            pltpu.VMEM((nhi, rows, cols), BF16),
+            pltpu.VMEM((nhi, rows, cols), BF16),
+            pltpu.VMEM((nhi - 1, 2, rows, cols), BF16),
+            pltpu.VMEM((nhi - 1, 2, rows, cols), BF16),
+            pltpu.VMEM((rows, cols), BF16),
+            pltpu.VMEM((rows, cols), BF16),
+            pltpu.VMEM((nhi - 1, rows, cols), BF16),
+            pltpu.VMEM((nhi - 1, rows, cols), BF16),
             pltpu.VMEM((subjects, cols), BF16),
             pltpu.VMEM((n, own_rows, ranks_one), F32),
             pltpu.VMEM((subjects, ranks_one), F32),
@@ -290,10 +343,12 @@
             dma((3,)),
             dma((CHUNKS,)),
             dma((CHUNKS,)),
-            dma((CHUNKS, chips - 1)),
-            dma((CHUNKS, chips - 1)),
-            dma((n - 1,)),
-            dma((n - 1,)),
+            dma((2,)),
+            dma((2,)),
+            dma((2, nhi - 1)),
+            dma((2, nhi - 1)),
+            dma((1 + nhi,)),
+            dma((1 + nhi,)),
             dma((n - 1,)),
             dma((n - 1,)),
         ],

time: 23.8 us -> 23.2 us (0.975)
  Pallas kernels: 22.3 us -> 21.8 us
    pallas_call x1, Pallas kernels: 22.3 us -> 21.8 us  [body(): pl.pallas_call(functools.partial(kernel, n), out_shape=jax.ShapeDtypeStru...]
where the time goes in v3:
time: 23.2 us; the launch traced here: 23.1 us
  Pallas kernels  21.8 us (94%)
  local copies, waits for them, and re-layouts  1.26 us (5%)
    pallas_call x1, Pallas kernels, body(): pl.pallas_call(functools.partial(kernel, n), out_shape=jax.ShapeDtypeStru...  21.8 us
    unnamed x1, local copies, waits for them, and re-layouts  1.26 us

profile of v3, /device:TPU:0, one launch (start us, length us, event | category | flops | bytes accessed | tf_op | source)
XLA Modules:
  0.0 23.1 jit_solution(8548181704994814645)
XLA Ops:
  0.0 21.8 %shard_map.46 = f32[4,128]{1,0:T(4,128)} custom-call(bf16[50,64,384]{2,1,0:T(8,128)(2,1)} %bitcast.2, bf16[16,50]{1,0:T(8,128)(2,1)} %bitcast.3, bf16[384,256]{1,0:T(8,128)(2,1)} %coord_hbm.1, bf16[4,128]{1,0:T(4,128)(2,1)} %subject_hbm.1), custom_call_target="tpu_custom_call" | custom-call | tf_op jit(solution)/shard_map/pallas_call | solution.py:315
  21.8 1.3 %copy.6 = f32[4,128]{1,0:T(4,128)} copy(f32[4,128]{1,0:T(4,128)} %shard_map.46) | data formatting | bytes 4096

commit v4 on v3

--- a/solution.py
+++ b/solution.py
@@ -11,7 +11,7 @@
 F32 = jnp.float32
 BF16 = jnp.bfloat16
 GROUP = 16
-LOADS = 4
+LOADS = 2
 CHUNKS = 2
 
 
@@ -140,9 +140,11 @@
     small[1].wait()
     coord_value = coord[...]
 
-    def compute(first):
+    def mix(first):
         block = data[:, first : first + GROUP, :].reshape(deep, width)
-        mixed = jnp.dot(weights, block, preferred_element_type=F32).astype(BF16)
+        return jnp.dot(weights, block, preferred_element_type=F32).astype(BF16)
+
+    def compute(first, mixed):
         term = jnp.dot(mixed, coord_value, preferred_element_type=F32)
         pieces = {}
         for q in range(ranks_two):
@@ -218,17 +220,22 @@
         for mask in range(n - 1, 0, -1)
     ]
 
+    small[2].wait()
+    factor_slots[me] = subject[...].astype(F32)
+    mixed = []
     for first in range(0, subjects, GROUP):
         if first % load_rows == 0:
             loads[first // load_rows].wait()
-        compute(first)
-    small[2].wait()
-    factor_slots[me] = subject[...].astype(F32)
-
-    pl.semaphore_wait(barrier, len(partners))
-    for copy in sibling_copies:
-        begin(copy)
-    begin(factor_sibling)
+        mixed.append((first, mix(first)))
+        if (first + GROUP) % rows == 0:
+            for item in mixed:
+                compute(*item)
+            mixed = []
+        if first + GROUP == rows:
+            pl.semaphore_wait(barrier, len(partners))
+            begin(sibling_copies[0])
+            begin(factor_sibling)
+    begin(sibling_copies[1])
     a = pl.ds(0, rows)
     b = pl.ds(rows, rows)
 

time: 23.2 us -> 21.2 us (0.914)
  Pallas kernels: 21.8 us -> 19.8 us
    pallas_call x1, Pallas kernels: 21.8 us -> 19.8 us  [body(): pl.pallas_call(functools.partial(kernel, n), out_shape=jax.ShapeDtypeStru...]
where the time goes in v4:
time: 21.2 us; the launch traced here: 21 us
  Pallas kernels  19.8 us (93%)
  local copies, waits for them, and re-layouts  1.26 us (6%)
    pallas_call x1, Pallas kernels, body(): pl.pallas_call(functools.partial(kernel, n), out_shape=jax.ShapeDtypeStru...  19.8 us
    unnamed x1, local copies, waits for them, and re-layouts  1.26 us

profile of v4, /device:TPU:0, one launch (start us, length us, event | category | flops | bytes accessed | tf_op | source)
XLA Modules:
  0.0 21.0 jit_solution(1372066215593069214)
XLA Ops:
  0.0 19.8 %shard_map.46 = f32[4,128]{1,0:T(4,128)} custom-call(bf16[50,64,384]{2,1,0:T(8,128)(2,1)} %bitcast.2, bf16[16,50]{1,0:T(8,128)(2,1)} %bitcast.3, bf16[384,256]{1,0:T(8,128)(2,1)} %coord_hbm.1, bf16[4,128]{1,0:T(4,128)(2,1)} %subject_hbm.1), custom_call_target="tpu_custom_call" | custom-call | tf_op jit(solution)/shard_map/pallas_call | solution.py:322
  19.8 1.3 %copy.6 = f32[4,128]{1,0:T(4,128)} copy(f32[4,128]{1,0:T(4,128)} %shard_map.46) | data formatting | bytes 4096
